TPU v7x, 32 devices: a whole 2x2x4 slice. The times are simulated.
32 devices in a mesh: block: 16 (over z, x, core), geo: 2 (over y).
Axes of the slice: x: 2, y: 2, z: 4, core: 2. Of those that a mesh axis runs over, the one named last changes fastest.
Arguments:
- admin_vectors: bfloat16 [131072, 256], P(('block', 'geo')), may hold values from -6 to 6
- admin_bucket: int32 [131072], P(('block', 'geo')), may hold values from 0 to 15
- admin_person_class: int32 [131072], P(('block', 'geo')), may hold values from 0 to 3
- admin_holder_bucket: int32 [131072, 1], P(('block', 'geo')), may hold values from 0 to 15; in each aligned block of 4096 rows (0 to 4095, 4096 to 8191, ...) at most 384 rows name the same one
- population_vectors: bfloat16 [16384, 256], P(('block', 'geo')), may hold values from -6 to 6
- population_bucket: int32 [16384], P(('block', 'geo')), may hold values from 0 to 15
- population_person_class: int32 [16384], P(('block', 'geo')), may hold values from 0 to 3
- model_coefficients: bfloat16 [256, 1024], replicated, may hold values from -0.375 to 0.375
Outputs:
- link_out: float32 [131072], P(('block', 'geo'))
- grad: float32 [256, 1024], P('block', 'geo')
Inputs may be any that keep to these rules, and one draw needn't show every extreme that they name: `admin_holder_bucket`: among the records of one device, no block index is named by more than 384 records.
All inputs are finite; a program needn't handle non-finite values.
Results may differ from a plain program's by a relative error of at most 0.00041.
Values may be sent and summed in bfloat16 or wider, within the bound.
A program may use at most 128 MiB of HBM per device.

v0:
```python
import jax
import jax.numpy as jnp
from jax import lax
from jax.sharding import PartitionSpec as P


def flipped_multiply(left, right):
    return lax.dot_general(
        left, right, (((0,), (0,)), ((), ())), preferred_element_type=jnp.float32
    )


def body(
    admin_vectors,
    admin_bucket,
    admin_person_class,
    admin_holder_bucket,
    population_vectors,
    population_bucket,
    population_person_class,
    model_coefficients,
):
    count = admin_vectors.shape[0]
    groups = lax.axis_size("block")
    regions = lax.axis_size("geo")
    capacity = 3 * count // (2 * groups)
    feat = admin_vectors.shape[1]
    hidden = model_coefficients.shape[1]
    normalizer = 1.0 / hidden**0.5
    dest = admin_holder_bucket[:, 0]
    onehot = (dest[:, None] == jnp.arange(groups, dtype=jnp.int32)[None, :]).astype(jnp.int32)
    order = jnp.sum((jnp.cumsum(onehot, axis=0) - 1) * onehot, axis=1)
    target = dest * capacity + order
    labels = jnp.stack([admin_bucket, admin_person_class], axis=1)
    send_meta = jnp.full((groups * capacity, 2), -1, jnp.int32).at[target].set(labels)
    send_meta = send_meta.reshape(groups, capacity, 2)
    population_mapped = jnp.dot(
        population_vectors, model_coefficients, preferred_element_type=jnp.float32
    ).astype(jnp.bfloat16)
    send_rows = jnp.zeros((groups * capacity, feat), jnp.bfloat16).at[target].set(admin_vectors)
    got_rows, got_meta = (
        lax.all_to_all(
            send_rows.reshape(groups, capacity, feat),
            "block",
            split_axis=0,
            concat_axis=0,
            tiled=True,
        ),
        lax.all_to_all(send_meta, "block", split_axis=0, concat_axis=0, tiled=True),
    )
    record_rows = got_rows.reshape(groups * capacity, feat)
    admin_descriptors = got_meta.reshape(groups * capacity, 2)
    mapped_entry = jnp.dot(
        record_rows, model_coefficients, preferred_element_type=jnp.float32
    ).astype(jnp.bfloat16)
    similarity = (
        jnp.dot(mapped_entry, population_mapped.T, preferred_element_type=jnp.float32) * normalizer
    )
    possible_couples = admin_descriptors[:, 0:1] == population_bucket[None, :]
    match_labels = (
        possible_couples & (admin_descriptors[:, 1:2] == population_person_class[None, :])
    ).astype(jnp.float32)
    prob = jax.nn.sigmoid(similarity)
    link = jnp.sum(jnp.where(possible_couples, prob, 0.0), axis=1)
    residual_error = jnp.where(possible_couples, prob - match_labels, 0.0).astype(jnp.bfloat16)
    admin_mapped_slope = (
        jnp.dot(residual_error, population_mapped, preferred_element_type=jnp.float32) * normalizer
    ).astype(jnp.bfloat16)
    population_mapped_slope = (flipped_multiply(residual_error, mapped_entry) * normalizer).astype(
        jnp.bfloat16
    )
    local_block = flipped_multiply(record_rows, admin_mapped_slope) + flipped_multiply(
        population_vectors, population_mapped_slope
    )
    returned = lax.all_to_all(
        link.reshape(groups, capacity), "block", split_axis=0, concat_axis=0, tiled=True
    )
    link_out = returned.reshape(-1)[target]
    local_block = local_block * (1.0 / (count * groups * regions) ** 0.5)
    rows_each = feat // groups
    cols_each = hidden // regions
    accumulated = lax.psum(local_block, ("block", "geo"))
    grad = lax.dynamic_slice(
        accumulated,
        (lax.axis_index("block") * rows_each, lax.axis_index("geo") * cols_each),
        (rows_each, cols_each),
    )
    return (link_out, grad)


def solution(mesh):
    placed = (
        P(("block", "geo"), None),
        P(("block", "geo")),
        P(("block", "geo")),
        P(("block", "geo"), None),
        P(("block", "geo"), None),
        P(("block", "geo")),
        P(("block", "geo")),
        P(),
    )
    return jax.shard_map(
        body,
        mesh=mesh,
        in_specs=placed,
        out_specs=(P(("block", "geo")), P("block", "geo")),
        check_vma=False,
    )
```

profile of v0, /device:TPU:0, one launch (start us, length us, event | category | flops | bytes accessed | tf_op | source)
XLA Modules:
  0.0 328.6 jit_solution(10269581285840515338)
XLA Ops:
  7.2 0.0 copy-start
  7.2 0.8 fusion.17
  8.0 4.6 %reduce-window.6 = s32[16,32,128]{2,1,0:T(8,128)S(1)} reduce-window(s32[16,32,128]{2,1,0:T(8,128)S(1)} %fusion.17, s32[]{:T(128)} %constant.17.clone.1), window={size=1x1x128 pad=0_0x0_0x127_0}, to_apply=%region_0.0 | reduce-window | flops 8323072 | bytes 524292 | tf_op jit(solution)/shard_map/reduce-window
  12.6 0.5 slice_reduce_fusion
  13.1 0.2 reduce-window.9
  13.3 0.1 add_add_fusion
  13.4 0.9 fusion.16
  14.3 0.7 compare_select_fusion.2
  15.1 0.8 pad_add_fusion
  15.8 0.6 copy.15
  16.5 12.4 %scatter_custom_fusion = s32[6144,2]{1,0:T(8,128)} fusion(s32[4096]{0:T(1024)S(1)} %bitcast.50, s32[4096,2]{1,0:T(8,128)S(1)} %copy.15, s32[]{:T(128)} %constant.15.clone.1), kind=kCustom, calls=%fused_computation.18 | custom fusion | bytes 49156 | tf_op jit(solution)/shard_map/scatter | solution.py:35
  28.9 0.0 copy-start.2
  28.9 3.0 copy.16
  31.9 7.4 %all-to-all-start = ((s32[16,384,2]{1,2,0:T(2,128)}), s32[16,384,2]{1,2,0:T(2,128)S(1)}, u32[]{:S(2)}, u32[]{:S(2)}) async-start(s32[16,384,2]{1,2,0:T(2,128)} %copy.16), calls=%async_computation | async-start | bytes 98304 | tf_op jit(solution)/shard_map/all_to_all | solution.py:49
  39.3 20.4 %scatter_custom_fusion.1 = bf16[6144,256]{1,0:T(8,128)(2,1)} fusion(s32[4096]{0:T(1024)S(1)} %bitcast.51, bf16[4096,256]{1,0:T(8,128)(2,1)} %param.8, bf16[]{:T(256)} %constant.20.clone.1), kind=kCustom, calls=%fused_computation.16 | custom fusion | bytes 3146240 | tf_op jit(solution)/shard_map/scatter | solution.py:40
  59.6 0.0 all-to-all-done
  59.7 6.1 %all-to-all-start.1 = ((bf16[16,384,256]{2,1,0:T(8,128)(2,1)}), bf16[16,384,256]{2,1,0:T(8,128)(2,1)}, u32[]{:S(2)}, u32[]{:S(2)}) async-start(bf16[16,384,256]{2,1,0:T(8,128)(2,1)} %bitcast.43), calls=%async_computation.1 | async-start | bytes 6291456 | tf_op jit(solution)/shard_map/all_to_all | solution.py:42
  65.7 0.2 all-reduce.2.cloned.1.call-start
  65.9 0.0 copy-done
  66.0 0.0 copy-done.2
  66.0 0.4 convolution_convert_fusion.1
  66.5 58.7 %all-to-all-done.1 = bf16[16,384,256]{2,1,0:T(8,128)(2,1)} async-done(((bf16[16,384,256]{2,1,0:T(8,128)(2,1)}), bf16[16,384,256]{2,1,0:T(8,128)(2,1)}, u32[]{:S(2)}, u32[]{:S(2)}) %all-to-all-start.1) | async-done | bytes 3145760 | tf_op jit(solution)/shard_map/all_to_all | solution.py:42
  125.1 0.0 copy-start.3
  125.1 0.0 copy-start.4
  125.1 5.5 %convolution_convert_fusion = bf16[6144,1024]{1,0:T(8,128)(2,1)S(1)} fusion(bf16[6144,256]{1,0:T(8,128)(2,1)} %bitcast.11, bf16[256,1024]{1,0:T(8,128)(2,1)S(1)} %copy-done), kind=kOutput, calls=%fused_computation.12 | convolution fusion | flops 3227516928 | bytes 16252928 | tf_op jit(solution)/shard_map/dot_general | solution.py:53
  130.7 0.0 copy-start.1
  130.7 0.0 copy-done.3
  130.7 0.0 copy-done.4
  130.7 21.9 %fusion.1 = (bf16[6144,512]{0,1:T(8,128)(2,1)}, f32[6144]{0:T(1024)}) fusion(s32[6144]{0:T(1024)S(1)} %bitcast.54, s32[6144]{0:T(1024)S(1)} %bitcast.55, s32[512]{0:T(512)S(1)} %copy-done.3, s32[512]{0:T(512)S(1)} %copy-done.4, bf16[6144,1024]{1,0:T(8,128)(2,1)S(1)} %convolution_convert_fusion, bf16[512,1024]{1,0:T(8,128)(2,1)S(1)} %convolution_convert_fusion.1), kind=kOutput, calls=%fused_computation.8 | convolution fusion | flops 6483339264 | bytes 20000768 | tf_op jit(solution)/shard_map/dot_general | solution.py:57
  152.6 0.0 copy-done.1
  152.6 12.1 %fusion.11 = f32[256,1024]{1,0:T(8,128)S(1)} fusion(bf16[512,256]{1,0:T(8,128)(2,1)S(1)} %copy-done.2, bf16[6144,512]{0,1:T(8,128)(2,1)} %get-tuple-element.2, bf16[6144,1024]{1,0:T(8,128)(2,1)} %copy-done.1), kind=kOutput, calls=%fused_computation.21 | convolution fusion | flops 6711934976 | bytes 20185088 | tf_op jit(solution)/shard_map/dot_general | solution.py:8
  164.8 14.7 %fusion.13 = f32[256,1024]{1,0:T(8,128)} fusion(f32[256,1024]{1,0:T(8,128)S(1)} %fusion.11, bf16[6144,256]{1,0:T(8,128)(2,1)} %bitcast.11, bf16[6144,512]{0,1:T(8,128)(2,1)} %get-tuple-element.2, bf16[512,1024]{1,0:T(8,128)(2,1)S(1)} %convolution_convert_fusion.1), kind=kOutput, calls=%fused_computation.23 | convolution fusion | flops 9676783616 | bytes 12582912 | tf_op jit(solution)/shard_map/dot_general | solution.py:8
  179.5 0.0 all-reduce.2.cloned.1.call-update
  179.5 15.4 %all-to-all-start.2 = ((f32[16,1,384]{2,1,0:T(1,128)}), f32[16,1,384]{2,1,0:T(1,128)S(1)}, u32[]{:S(2)}, u32[]{:S(2)}) async-start(f32[16,1,384]{2,1,0:T(1,128)} %bitcast.12), calls=%async_computation.2 | async-start | bytes 49152 | tf_op jit(solution)/shard_map/all_to_all | solution.py:75
  195.0 6.6 %all-to-all-done.2 = f32[16,1,384]{2,1,0:T(1,128)S(1)} async-done(((f32[16,1,384]{2,1,0:T(1,128)}), f32[16,1,384]{2,1,0:T(1,128)S(1)}, u32[]{:S(2)}, u32[]{:S(2)}) %all-to-all-start.2) | async-done | bytes 24608 | tf_op jit(solution)/shard_map/all_to_all | solution.py:75
  201.5 40.5 %gather_fusion = f32[4096]{0:T(1024)} fusion(f32[6144]{0:T(1024)S(1)} %bitcast.42, s32[4096]{0:T(1024)S(1)} %broadcast_clamp_fusion), kind=kCustom, calls=%fused_computation | custom fusion | bytes 49152 | tf_op jit(solution)/shard_map/gather | solution.py:78
  242.1 78.3 %all-reduce.2.cloned.1.call-done = f32[256,1024]{1,0:T(8,128)} async-done(((f32[256,1024]{1,0:T(8,128)}), f32[256,1024]{1,0:T(8,128)}) %all-reduce.2.cloned.1.call-update) | async-done | bytes 1048592 | tf_op jit(solution)/shard_map/psum | solution.py:82
  320.4 1.4 dynamic_slice.3
  (2 shorter events, 0.0 us)
Async XLA Ops:
  7.2 58.8 %copy-start = (bf16[256,1024]{1,0:T(8,128)(2,1)S(1)}, bf16[256,1024]{1,0:T(8,128)(2,1)}, u32[]{:S(2)}) copy-start(bf16[256,1024]{1,0:T(8,128)(2,1)} %param.15) | copy-start | bytes 1572868
  28.9 37.0 %copy-start.2 = (bf16[512,256]{1,0:T(8,128)(2,1)S(1)}, bf16[512,256]{1,0:T(8,128)(2,1)}, u32[]{:S(2)}) copy-start(bf16[512,256]{1,0:T(8,128)(2,1)} %param.12) | copy-start | bytes 786436
  31.9 27.7 %all-to-all-start = ((s32[16,384,2]{1,2,0:T(2,128)}), s32[16,384,2]{1,2,0:T(2,128)S(1)}, u32[]{:S(2)}, u32[]{:S(2)}) async-start(s32[16,384,2]{1,2,0:T(2,128)} %copy.16), calls=%async_computation | async-start | bytes 98304 | tf_op jit(solution)/shard_map/all_to_all | solution.py:49
  59.7 65.5 %all-to-all-start.1 = ((bf16[16,384,256]{2,1,0:T(8,128)(2,1)}), bf16[16,384,256]{2,1,0:T(8,128)(2,1)}, u32[]{:S(2)}, u32[]{:S(2)}) async-start(bf16[16,384,256]{2,1,0:T(8,128)(2,1)} %bitcast.43), calls=%async_computation.1 | async-start | bytes 6291456 | tf_op jit(solution)/shard_map/all_to_all | solution.py:42
  65.7 254.6 %all-reduce.2.cloned.1.call-start = ((), (), s32[]{:S(2)}) async-start(), calls=%async_computation.3 | async-start | bytes 2097152 | tf_op jit(solution)/shard_map/psum | solution.py:82
  125.1 5.6 %copy-start.3 = (s32[512]{0:T(512)S(1)}, s32[512]{0:T(512)}, u32[]{:S(2)}) copy-start(s32[512]{0:T(512)} %param.14) | copy-start | bytes 6148
  125.1 5.6 %copy-start.4 = (s32[512]{0:T(512)S(1)}, s32[512]{0:T(512)}, u32[]{:S(2)}) copy-start(s32[512]{0:T(512)} %param.13) | copy-start | bytes 6148
  130.7 22.0 %copy-start.1 = (bf16[6144,1024]{1,0:T(8,128)(2,1)}, bf16[6144,1024]{1,0:T(8,128)(2,1)S(1)}, u32[]{:S(2)}) copy-start(bf16[6144,1024]{1,0:T(8,128)(2,1)S(1)} %convolution_convert_fusion) | copy-start | bytes 37748740
  179.5 22.0 %all-to-all-start.2 = ((f32[16,1,384]{2,1,0:T(1,128)}), f32[16,1,384]{2,1,0:T(1,128)S(1)}, u32[]{:S(2)}, u32[]{:S(2)}) async-start(f32[16,1,384]{2,1,0:T(1,128)} %bitcast.12), calls=%async_computation.2 | async-start | bytes 49152 | tf_op jit(solution)/shard_map/all_to_all | solution.py:75
Sparse Core Ops, SparseCore 0:
  179.6 140.6 all-reduce.1
where the time goes:
time: 329 us
  waiting for transfers between devices  144 us (44%)
  local copies, waits for them, and re-layouts  78.9 us (24%)
  matrix products  54.7 us (17%)
  starting transfers between devices  29.1 us (9%)
  between operations  14.2 us (4%)
  other arithmetic  8.16 us (2%)
    psum x1, waiting for transfers between devices, body(): accumulated = lax.psum(local_block, ('block', 'geo'))  78.3 us
    all_to_all x1, waiting for transfers between devices, body(): lax.all_to_all(send_rows.reshape(groups, capacity, feat), 'block', split_...  58.7 us
    gather x1, local copies, waits for them, and re-layouts, body(): link_out = returned.reshape(-1)[target]  40.5 us
    dot_general x2, matrix products, flipped_multiply(): lax.dot_general(left, right, (((0,), (0,)), ((), ())), preferred_element_...  26.8 us
    dot_general x1, matrix products, body(): jnp.dot(mapped_entry, population_mapped.T, preferred_element_type=jnp.flo...  21.9 us
    scatter x1, local copies, waits for them, and re-layouts, body(): jnp.zeros((groups * capacity, feat), jnp.bfloat16).at[target]  20.4 us
    all_to_all x1, starting transfers between devices, body(): lax.all_to_all(link.reshape(groups, capacity), 'block', split_axis=0, con...  15.4 us
    scatter x1, local copies, waits for them, and re-layouts, body(): jnp.full((groups * capacity, 2), -1, jnp.int32).at[target].set(labels)  12.4 us
  transfers between devices with their start and end apart: 4, of which 3 were waited for; matrix products, arithmetic and copies ran while one was open for 19% of the time, Pallas kernels for 0%

commit v1 on v0

v1 whole, which is shorter than its diff:
```python
import functools

import jax
import jax.numpy as jnp
from jax import lax
from jax.experimental import pallas as pl
from jax.experimental.pallas import tpu as pltpu
from jax.sharding import PartitionSpec as P

F32 = jnp.float32
BF16 = jnp.bfloat16
LANES = 512


def over_rows(left, right):
    return lax.dot_general(left, right, (((0,), (0,)), ((), ())), preferred_element_type=F32)


def over_columns(left, right):
    return lax.dot_general(left, right, (((1,), (1,)), ((), ())), preferred_element_type=F32)


def plain(left, right):
    return jnp.dot(left, right, preferred_element_type=F32)


def order_kernel(groups, cap, dest_ref, code_ref, x_ref, m_ref, proj_ref, rows_ref, slots_ref, rank_ref):
    owner = pl.program_id(0)
    count = dest_ref.shape[1]

    @pl.when(owner == 0)
    def _():
        width = 256
        before = lax.broadcasted_iota(jnp.int32, (width, width), 0)
        after = lax.broadcasted_iota(jnp.int32, (width, width), 1)
        upper = jnp.where(before <= after, 1.0, 0.0).astype(BF16)
        carry = jnp.zeros((groups, 1), F32)
        slots = jnp.zeros((groups, cap), F32)
        for at in range(0, count, width):
            span = pl.ds(at, width)
            owners = lax.broadcasted_iota(jnp.int32, (groups, width), 0)
            onehot = jnp.where(owners == dest_ref[:, span], 1.0, 0.0)
            running = plain(onehot.astype(BF16), upper) + carry
            rank = (jnp.sum(running * onehot, axis=0, keepdims=True) - 1.0).astype(jnp.int32)
            rank_ref[:, span] = rank
            carry = running[:, width - 1 : width]
            places = lax.broadcasted_iota(jnp.int32, (cap, width), 0)
            placed = jnp.where(places == rank, 1.0, 0.0).astype(BF16)
            slots = slots + over_columns((onehot * code_ref[:, span]).astype(BF16), placed)
        slots_ref[...] = slots

    rows = jnp.zeros((cap, x_ref.shape[1]), F32)
    places = lax.broadcasted_iota(jnp.int32, (cap, LANES), 0)
    for at in range(0, count, LANES):
        span = pl.ds(at, LANES)
        mine = jnp.where(dest_ref[:, span] == owner, rank_ref[:, span], -1)
        placed = jnp.where(places == mine, 1.0, 0.0).astype(BF16)
        rows = rows + plain(placed, x_ref[span, :])
    rows = rows.astype(BF16)
    rows_ref[0] = rows
    proj_ref[0] = plain(rows, m_ref[...]).astype(BF16)


def score_kernel(
    groups, cap, grad_scale,
    dest_ref, rank_ref, slots_ref, m_ref, proj_ref, rows_ref, census_ref,
    link_ref, sym_ref, total_ref, sums_ref,
):
    owner = pl.program_id(0)
    count = dest_ref.shape[1]
    feat = rows_ref.shape[2]
    hidden = m_ref.shape[1]
    people = census_ref.shape[1] // 16 * 16 - 16

    census = census_ref[0, :people, :]
    labels = census_ref[0, people:, :].astype(F32)
    columns = []
    for part in range(people // feat):
        row = jnp.broadcast_to(labels[part : part + 1, :], (128, feat))
        columns.append(jnp.transpose(row)[:, :1])
    label = jnp.concatenate(columns, axis=0)
    key = jnp.floor((label - 1.0) * 0.25)
    slot_label = slots_ref[pl.ds(owner, 1), :]
    slot_key = jnp.floor((slot_label - 1.0) * 0.25)

    mapped = plain(census, m_ref[...]).astype(BF16)
    raw = over_columns(mapped, proj_ref[0])
    prob = 0.5 * jnp.tanh(raw * (0.5 / hidden**0.5)) + 0.5
    prob = jnp.where(key == slot_key, prob, 0.0)
    sums_ref[pl.ds(owner, 1), :] = jnp.sum(prob, axis=0, keepdims=True)
    resid = (prob - jnp.where(label == slot_label, 1.0, 0.0)).astype(BF16)
    pulled = plain(resid, rows_ref[0])
    high = pulled.astype(BF16)
    low = (pulled - high.astype(F32)).astype(BF16)
    step = over_rows(census, high) + over_rows(census, low)

    @pl.when(owner == 0)
    def _():
        total_ref[...] = step

    @pl.when(owner > 0)
    def _():
        total_ref[...] += step

    @pl.when(owner == groups - 1)
    def _():
        total = total_ref[...]
        sym_ref[...] = (total + jnp.transpose(total)) * grad_scale
        sums = sums_ref[...]
        top = sums.astype(BF16)
        rest = (sums - top.astype(F32)).astype(BF16)
        places = lax.broadcasted_iota(jnp.int32, (cap, LANES), 0)
        owners = lax.broadcasted_iota(jnp.int32, (groups, LANES), 0)
        for at in range(0, count, LANES):
            span = pl.ds(at, LANES)
            onehot = jnp.where(owners == dest_ref[:, span], 1.0, 0.0).astype(BF16)
            spread = over_rows(top, onehot) + over_rows(rest, onehot)
            spread = jnp.where(places == rank_ref[:, span], spread, 0.0)
            link_ref[:, span] = jnp.sum(spread, axis=0, keepdims=True)


def body(
    admin_vectors,
    admin_bucket,
    admin_person_class,
    admin_holder_bucket,
    population_vectors,
    population_bucket,
    population_person_class,
    model_coefficients,
):
    count, feat = admin_vectors.shape
    groups = lax.axis_size("block")
    regions = lax.axis_size("geo")
    cap = 3 * count // (2 * groups)
    hidden = model_coefficients.shape[1]
    people = population_vectors.shape[0]
    dest = admin_holder_bucket.reshape(1, count)
    code = (admin_bucket * 4 + admin_person_class + 1).astype(F32).reshape(1, count)
    census_code = (population_bucket * 4 + population_person_class + 1).astype(BF16)
    census_code = census_code.reshape(people // feat, feat)
    census_code = jnp.pad(census_code, ((0, 16 - people // feat), (0, 0)))
    census = lax.all_gather(jnp.concatenate([population_vectors, census_code], axis=0), "block")
    tall = people + 16

    def whole(shape):
        return pl.BlockSpec(shape, lambda o: (0,) * len(shape))

    def each(shape):
        return pl.BlockSpec((1,) + shape, lambda o: (o, 0, 0))

    proj, rows, slots, rank = pl.pallas_call(
        functools.partial(order_kernel, groups, cap),
        grid=(groups,),
        in_specs=[whole((1, count)), whole((1, count)), whole((count, feat)), whole((feat, hidden))],
        out_specs=[each((cap, hidden)), each((cap, feat)), whole((groups, cap)), whole((1, count))],
        out_shape=[
            jax.ShapeDtypeStruct((groups, cap, hidden), BF16),
            jax.ShapeDtypeStruct((groups, cap, feat), BF16),
            jax.ShapeDtypeStruct((groups, cap), F32),
            jax.ShapeDtypeStruct((1, count), jnp.int32),
        ],
        compiler_params=pltpu.CompilerParams(vmem_limit_bytes=40 << 20),
        cost_estimate=pl.CostEstimate(
            flops=2 * groups * cap * feat * (count + hidden), bytes_accessed=20 << 20, transcendentals=0
        ),
        name="order_records",
    )(dest, code, admin_vectors, model_coefficients)

    grad_scale = 1.0 / hidden**0.5 / (count * groups * regions) ** 0.5
    link, sym = pl.pallas_call(
        functools.partial(score_kernel, groups, cap, grad_scale),
        grid=(groups,),
        in_specs=[
            whole((1, count)),
            whole((1, count)),
            whole((groups, cap)),
            whole((feat, hidden)),
            each((cap, hidden)),
            each((cap, feat)),
            each((tall, feat)),
        ],
        out_specs=[whole((1, count)), whole((feat, feat))],
        out_shape=[jax.ShapeDtypeStruct((1, count), F32), jax.ShapeDtypeStruct((feat, feat), F32)],
        scratch_shapes=[pltpu.VMEM((feat, feat), F32), pltpu.VMEM((groups, cap), F32)],
        compiler_params=pltpu.CompilerParams(vmem_limit_bytes=40 << 20),
        cost_estimate=pl.CostEstimate(
            flops=2 * groups * people * (feat * hidden + cap * hidden + cap * feat + 2 * feat * feat),
            bytes_accessed=20 << 20,
            transcendentals=groups * people * cap,
        ),
        name="score_pairs",
    )(dest, rank, slots, model_coefficients, proj, rows, census)

    sym = lax.psum(sym, ("block", "geo"))
    rows_each = feat // groups
    cols_each = hidden // regions
    mine = lax.dynamic_slice(sym, (lax.axis_index("block") * rows_each, 0), (rows_each, feat))
    model = lax.dynamic_slice(
        model_coefficients, (0, lax.axis_index("geo") * cols_each), (feat, cols_each)
    )
    grad = jnp.dot(mine, model.astype(F32), precision=lax.Precision.HIGHEST)
    return (link.reshape(count), grad)


def solution(mesh):
    placed = (
        P(("block", "geo"), None),
        P(("block", "geo")),
        P(("block", "geo")),
        P(("block", "geo"), None),
        P(("block", "geo"), None),
        P(("block", "geo")),
        P(("block", "geo")),
        P(),
    )
    return jax.shard_map(
        body,
        mesh=mesh,
        in_specs=placed,
        out_specs=(P(("block", "geo")), P("block", "geo")),
        check_vma=False,
    )
```

time: 329 us -> 232 us (0.71)
  local copies, waits for them, and re-layouts: 78.9 us -> 9.13 us
  Pallas kernels: 0 us -> 60.9 us
  matrix products: 54.7 us -> 1.55 us
  starting transfers between devices: 29.1 us -> 0.08 us
  other arithmetic: 8.16 us -> 3.11 us
    all_to_all x3 -> x0, waiting for transfers between devices: 65.2 us -> none  [the longest x1 58.7 us: body(): lax.all_to_all(send_rows.reshape(groups, capacity, feat), 'block', split_...]
    pallas_call x0 -> x2, Pallas kernels: none -> 60.9 us  [the longest x1 30.8 us: body(): pl.pallas_call(functools.partial(score_kernel, groups, cap, grad_scale),...]
    dot_general x5 -> x1, matrix products: 54.7 us -> 1.55 us  [body(): grad = jnp.dot(mine, model.astype(F32), precision=lax.Precision.HIGHEST)]
    psum x1, waiting for transfers between devices: 78.3 us -> 124 us  [body(): sym = lax.psum(sym, ('block', 'geo'))]
    gather x1 -> x0, local copies, waits for them, and re-layouts: 40.5 us -> none  [body(): link_out = returned.reshape(-1)[target]]
    scatter x2 -> x0, local copies, waits for them, and re-layouts: 32.8 us -> none  [the longest x1 20.4 us: body(): jnp.zeros((groups * capacity, feat), jnp.bfloat16).at[target]]
    all_to_all x3 -> x0, starting transfers between devices: 28.8 us -> none  [the longest x1 15.4 us: body(): lax.all_to_all(link.reshape(groups, capacity), 'block', split_axis=0, con...]
    all_gather x0 -> x1, waiting for transfers between devices: none -> 18.8 us  [body(): lax.all_gather(jnp.concatenate([population_vectors, census_code], axis=0)...]
  transfers between devices with their start and end apart: 4 -> 2, of which waited for: 3 -> 2; matrix products, arithmetic and copies ran while one was open for 19% -> 0% of each run, Pallas kernels for 0% -> 13%
where the time goes in v1:
time: 232 us; the launch traced here: 231 us
  waiting for transfers between devices  142 us (61%)
  Pallas kernels  60.9 us (26%)
  between operations  14.1 us (6%)
  local copies, waits for them, and re-layouts  9.13 us (4%)
  other arithmetic  3.11 us (1%)
    psum x1, waiting for transfers between devices, body(): sym = lax.psum(sym, ('block', 'geo'))  124 us
    pallas_call x1, Pallas kernels, body(): pl.pallas_call(functools.partial(score_kernel, groups, cap, grad_scale),...  30.8 us
    pallas_call x1, Pallas kernels, body(): pl.pallas_call(functools.partial(order_kernel, groups, cap), grid=(groups...  30.1 us
    all_gather x1, waiting for transfers between devices, body(): lax.all_gather(jnp.concatenate([population_vectors, census_code], axis=0)...  18.8 us
    unnamed x16, local copies, waits for them, and re-layouts  9.12 us
  transfers between devices with their start and end apart: 2, of which 2 were waited for; matrix products, arithmetic and copies ran while one was open for 0% of the time, Pallas kernels for 13%

profile of v1, /device:TPU:0, one launch (start us, length us, event | category | flops | bytes accessed | tf_op | source)
XLA Modules:
  0.0 231.3 jit_solution(13343956010060247771)
XLA Ops:
  7.2 0.0 all-gather.3.cloned.1.call-start
  7.2 0.7 add_convert_fusion.1
  7.9 1.7 fusion.1
  9.6 0.0 all-gather.3.cloned.1.call-update
  9.6 0.0 all-reduce.3.cloned.1.call-start
  9.7 0.7 add_convert_fusion
  10.4 0.0 copy-start
  10.4 1.0 copy-done
  11.5 0.0 copy-start.3
  11.5 1.6 copy-done.3
  13.1 0.0 copy-start.4
  13.1 0.7 copy-done.4
  13.8 0.0 copy-start.1
  13.8 0.0 copy-start.5
  13.8 30.1 %order_records.1 = (bf16[16,384,1024]{2,1,0:T(8,128)(2,1)}, bf16[16,384,256]{2,1,0:T(8,128)(2,1)S(1)}, f32[16,384]{1,0:T(8,128)S(1)}, s32[1,4096]{1,0:T(1,128)S(1)}) custom-call(s32[1,4096]{1,0:T(1,128)S(1)} %bitcast.6, f32[1,4096]{1,0:T(1,128)S(1)} %bitcast.4, bf16[4096,256]{1,0:T(8,128)(2,1)S(1)} %copy-done.3, bf16[256,1024]{1,0:T(8,128)(2,1)S(1)} %copy-done), custom_call_target="tpu_custom_call" | custom-call | flops 16106127360 | bytes 20971520 | tf_op jit(solution)/shard_map/order_records/pallas_call | solution.py:152
  43.8 0.0 copy-start.6
  43.8 1.6 copy-done.6
  45.5 18.8 %all-gather.3.cloned.1.call-done = bf16[8448,256]{1,0:T(8,128)(2,1)} async-done(((bf16[528,256]{1,0:T(8,128)(2,1)}), bf16[8448,256]{1,0:T(8,128)(2,1)}) %all-gather.3.cloned.1.call-update) | async-done | bytes 4325392 | tf_op jit(solution)/shard_map/all_gather | solution.py:143
  64.3 0.0 copy-done.1
  64.3 0.0 copy-done.5
  64.3 0.0 copy-start.2
  64.3 2.2 copy-done.2
  66.5 0.0 copy-start.7
  66.5 1.9 copy-done.7
  68.4 30.8 %score_pairs.1 = (f32[1,4096]{1,0:T(1,128)}, f32[256,256]{1,0:T(8,128)}) custom-call(s32[1,4096]{1,0:T(1,128)S(1)} %bitcast.7, s32[1,4096]{1,0:T(1,128)S(1)} %get-tuple-element.8.rank_ref, f32[16,384]{1,0:T(8,128)S(1)} %get-tuple-element.9.slots_ref, bf16[256,1024]{1,0:T(8,128)(2,1)S(1)} %copy-done.1, bf16[16,384,1024]{2,1,0:T(8,128)(2,1)} %get-tuple-element.10.proj_ref, ...), custom_call_target="tpu_custom_call" | custom-call | flops 14495514624 | bytes 20971520 | tf_op jit(solution)/shard_map/score_pairs/pallas_call | solution.py:171
  99.2 0.0 all-reduce.3.cloned.1.call-update
  99.2 123.7 %all-reduce.3.cloned.1.call-done = f32[256,256]{1,0:T(8,128)} async-done(((f32[256,256]{1,0:T(8,128)}), f32[256,256]{1,0:T(8,128)}) %all-reduce.3.cloned.1.call-update) | async-done | bytes 262160 | tf_op jit(solution)/shard_map/psum | solution.py:195
  222.9 1.6 fusion.2
  (1 shorter events, 0.0 us)
Async XLA Ops:
  7.2 57.1 %all-gather.3.cloned.1.call-start = ((), (), s32[]{:S(2)}) async-start(), calls=%async_computation.1 | async-start | bytes 4595712 | tf_op jit(solution)/shard_map/all_gather | solution.py:143
  9.6 213.3 %all-reduce.3.cloned.1.call-start = ((), (), s32[]{:S(2)}) async-start(), calls=%async_computation | async-start | bytes 524288 | tf_op jit(solution)/shard_map/psum | solution.py:195
  10.4 1.0 copy-start
  11.5 1.6 copy-start.3
  13.1 0.7 copy-start.4
  13.8 50.5 %copy-start.1 = (bf16[256,1024]{1,0:T(8,128)(2,1)S(1)}, bf16[256,1024]{1,0:T(8,128)(2,1)}, u32[]{:S(2)}) copy-start(bf16[256,1024]{1,0:T(8,128)(2,1)} %m_ref.3) | copy-start | bytes 1572868
  13.8 50.5 %copy-start.5 = (s32[4096,1]{0,1:T(1,128)S(1)}, s32[4096,1]{0,1:T(1,128)}, u32[]{:S(2)}) copy-start(s32[4096,1]{0,1:T(1,128)} %param.11) | copy-start | bytes 49156
  43.8 1.6 copy-start.6
  64.3 2.2 copy-start.2
  66.5 1.9 copy-start.7
Sparse Core Ops, SparseCore 0:
  10.3 53.9 all-gather.2
  99.3 123.5 all-reduce.2

commit v2 on v1

--- a/solution.py
+++ b/solution.py
@@ -10,6 +10,7 @@
 F32 = jnp.float32
 BF16 = jnp.bfloat16
 LANES = 512
+MESH = pl.DeviceIdType.MESH
 
 
 def over_rows(left, right):
@@ -24,9 +25,102 @@
     return jnp.dot(left, right, preferred_element_type=F32)
 
 
-def order_kernel(groups, cap, dest_ref, code_ref, x_ref, m_ref, proj_ref, rows_ref, slots_ref, rank_ref):
+def gather_plan(groups, own_ref, all_ref, send1, recv1, send2, recv2, send3, recv3):
+    outer, inner = 4, groups // 8
+    block = lax.axis_index("block")
+    core = lax.rem(block, 2)
+    x = lax.rem(block // 2, inner)
+    z = block // (2 * inner)
+
+    def number(z, x, core):
+        return (z * inner + x) * 2 + core
+
+    def held(k, j):
+        if k == 0 and j == 0:
+            return own_ref
+        return all_ref.at[number(lax.rem(z + outer - k, outer), lax.rem(x + inner - j, inner), core)]
+
+    def slot(k, j):
+        return all_ref.at[number(lax.rem(z + outer - k, outer), lax.rem(x + inner - j, inner), core)]
+
+    def copy(source, target, send, recv, peer):
+        return pltpu.make_async_remote_copy(
+            src_ref=source, dst_ref=target, send_sem=send, recv_sem=recv,
+            device_id={"block": peer}, device_id_type=MESH,
+        )
+
+    peers = [number(lax.rem(z + k, outer), x, core) for k in range(1, outer)]
+    peers += [number(z, lax.rem(x + j, inner), core) for j in range(1, inner)]
+    peers += [number(z, x, 1 - core)]
+
+    def along_outer(k):
+        return copy(own_ref, slot(0, 0), send1.at[k], recv1.at[k], peers[k - 1])
+
+    def along_inner(k, j):
+        at = k * inner + j
+        return copy(held(k, 0), slot(k, 0), send2.at[at], recv2.at[at], number(z, lax.rem(x + j, inner), core))
+
+    def to_core(k, j):
+        at = k * inner + j
+        return copy(held(k, j), slot(k, j), send3.at[at], recv3.at[at], peers[-1])
+
+    return outer, inner, block, peers, along_outer, along_inner, to_core
+
+
+def gather_step(groups, step, own_ref, all_ref, local, *sems):
+    outer, inner, block, peers, along_outer, along_inner, to_core = gather_plan(
+        groups, own_ref, all_ref, *sems
+    )
+
+    @pl.when(step == 0)
+    def _():
+        barrier = pltpu.get_barrier_semaphore()
+        for peer in peers:
+            pl.semaphore_signal(barrier, inc=1, device_id={"block": peer}, device_id_type=MESH)
+        pl.semaphore_wait(barrier, len(peers))
+        for k in (2, 3, 1):
+            along_outer(k).start()
+        for j in range(1, inner):
+            along_inner(0, j).start()
+        to_core(0, 0).start()
+        pltpu.make_async_copy(own_ref, all_ref.at[block], local).start()
+
+    for k in range(1, outer):
+
+        @pl.when(step == (2, 6, 8, 10)[k])
+        def _(k=k):
+            along_outer(k).wait_recv()
+            for j in range(1, inner):
+                along_inner(k, j).start()
+            to_core(k, 0).start()
+
+    for k in range(outer):
+
+        @pl.when(step == (7, 10, 12, 14)[k])
+        def _(k=k):
+            for j in range(1, inner):
+                along_inner(k, j).wait_recv()
+                to_core(k, j).start()
+
+    @pl.when(step == groups - 1)
+    def _():
+        pltpu.make_async_copy(own_ref, all_ref.at[block], local).wait()
+        for k in range(1, outer):
+            along_outer(k).wait_send()
+        for k in range(outer):
+            for j in range(1, inner):
+                along_inner(k, j).wait_send()
+            for j in range(inner):
+                to_core(k, j).wait()
+
+
+def order_kernel(
+    groups, cap, dest_ref, code_ref, x_ref, m_ref, own_ref, proj_ref, rows_ref, slots_ref, rank_ref, all_ref,
+    local, *sems,
+):
     owner = pl.program_id(0)
     count = dest_ref.shape[1]
+    gather_step(groups, owner, own_ref, all_ref, local, *sems)
 
     @pl.when(owner == 0)
     def _():
@@ -117,6 +211,65 @@
             spread = over_rows(top, onehot) + over_rows(rest, onehot)
             spread = jnp.where(places == rank_ref[:, span], spread, 0.0)
             link_ref[:, span] = jnp.sum(spread, axis=0, keepdims=True)
+
+
+def reduce_kernel(groups, regions, sym_ref, m_ref, grad_ref, got, mid, send1, recv1, send2, recv2):
+    block = lax.axis_index("block")
+    region = lax.axis_index("geo")
+    rows = got.shape[1]
+    cols = grad_ref.shape[1]
+    barrier = pltpu.get_barrier_semaphore()
+    for k in range(1, groups):
+        pl.semaphore_signal(
+            barrier, inc=1, device_id={"block": lax.rem(block + k, groups)}, device_id_type=MESH
+        )
+    for k in range(1, regions):
+        pl.semaphore_signal(
+            barrier, inc=1, device_id={"geo": lax.rem(region + k, regions)}, device_id_type=MESH
+        )
+    pl.semaphore_wait(barrier, groups + regions - 2)
+
+    copies = []
+    for k in range(1, groups):
+        peer = lax.rem(block + k, groups)
+        copy = pltpu.make_async_remote_copy(
+            src_ref=sym_ref.at[pl.ds(pl.multiple_of(peer * rows, rows), rows), :],
+            dst_ref=got.at[k],
+            send_sem=send1.at[k],
+            recv_sem=recv1.at[k],
+            device_id={"block": peer},
+            device_id_type=MESH,
+        )
+        copy.start()
+        copies.append(copy)
+    total = sym_ref[pl.ds(pl.multiple_of(block * rows, rows), rows), :]
+    for k in range(1, groups):
+        copies[k - 1].wait_recv()
+        total = total + got[k]
+    mid[0] = total
+    crossing = []
+    for k in range(1, regions):
+        copy = pltpu.make_async_remote_copy(
+            src_ref=mid.at[0],
+            dst_ref=mid.at[k],
+            send_sem=send2.at[k],
+            recv_sem=recv2.at[k],
+            device_id={"geo": lax.rem(region + k, regions)},
+            device_id_type=MESH,
+        )
+        copy.start()
+        crossing.append(copy)
+    for k in range(1, regions):
+        crossing[k - 1].wait_recv()
+        total = total + mid[k]
+    model = m_ref[:, pl.ds(pl.multiple_of(region * cols, cols), cols)]
+    first = total.astype(BF16)
+    left = total - first.astype(F32)
+    second = left.astype(BF16)
+    third = (left - second.astype(F32)).astype(BF16)
+    grad_ref[...] = plain(first, model) + plain(second, model) + plain(third, model)
+    for copy in copies + crossing:
+        copy.wait_send()
 
 
 def body(
@@ -140,7 +293,7 @@
     census_code = (population_bucket * 4 + population_person_class + 1).astype(BF16)
     census_code = census_code.reshape(people // feat, feat)
     census_code = jnp.pad(census_code, ((0, 16 - people // feat), (0, 0)))
-    census = lax.all_gather(jnp.concatenate([population_vectors, census_code], axis=0), "block")
+    census = jnp.concatenate([population_vectors, census_code], axis=0)
     tall = people + 16
 
     def whole(shape):
@@ -149,23 +302,31 @@
     def each(shape):
         return pl.BlockSpec((1,) + shape, lambda o: (o, 0, 0))
 
-    proj, rows, slots, rank = pl.pallas_call(
+    proj, rows, slots, rank, census = pl.pallas_call(
         functools.partial(order_kernel, groups, cap),
         grid=(groups,),
-        in_specs=[whole((1, count)), whole((1, count)), whole((count, feat)), whole((feat, hidden))],
-        out_specs=[each((cap, hidden)), each((cap, feat)), whole((groups, cap)), whole((1, count))],
+        in_specs=[whole((1, count)), whole((1, count)), whole((count, feat)), whole((feat, hidden))]
+        + [pl.BlockSpec(memory_space=pl.ANY)],
+        out_specs=[each((cap, hidden)), each((cap, feat)), whole((groups, cap)), whole((1, count))]
+        + [pl.BlockSpec(memory_space=pl.ANY)],
         out_shape=[
             jax.ShapeDtypeStruct((groups, cap, hidden), BF16),
             jax.ShapeDtypeStruct((groups, cap, feat), BF16),
             jax.ShapeDtypeStruct((groups, cap), F32),
             jax.ShapeDtypeStruct((1, count), jnp.int32),
+            jax.ShapeDtypeStruct((groups, tall, feat), BF16),
         ],
-        compiler_params=pltpu.CompilerParams(vmem_limit_bytes=40 << 20),
+        scratch_shapes=[pltpu.SemaphoreType.DMA]
+        + [pltpu.SemaphoreType.DMA((4,))] * 2
+        + [pltpu.SemaphoreType.DMA((groups // 2,))] * 4,
+        compiler_params=pltpu.CompilerParams(
+            vmem_limit_bytes=40 << 20, collective_id=1, has_side_effects=True
+        ),
         cost_estimate=pl.CostEstimate(
             flops=2 * groups * cap * feat * (count + hidden), bytes_accessed=20 << 20, transcendentals=0
         ),
         name="order_records",
-    )(dest, code, admin_vectors, model_coefficients)
+    )(dest, code, admin_vectors, model_coefficients, census)
 
     grad_scale = 1.0 / hidden**0.5 / (count * groups * regions) ** 0.5
     link, sym = pl.pallas_call(
@@ -192,14 +353,27 @@
         name="score_pairs",
     )(dest, rank, slots, model_coefficients, proj, rows, census)
 
-    sym = lax.psum(sym, ("block", "geo"))
     rows_each = feat // groups
     cols_each = hidden // regions
-    mine = lax.dynamic_slice(sym, (lax.axis_index("block") * rows_each, 0), (rows_each, feat))
-    model = lax.dynamic_slice(
-        model_coefficients, (0, lax.axis_index("geo") * cols_each), (feat, cols_each)
-    )
-    grad = jnp.dot(mine, model.astype(F32), precision=lax.Precision.HIGHEST)
+    grad = pl.pallas_call(
+        functools.partial(reduce_kernel, groups, regions),
+        in_specs=[pl.BlockSpec(memory_space=pltpu.VMEM)] * 2,
+        out_specs=pl.BlockSpec(memory_space=pltpu.VMEM),
+        out_shape=jax.ShapeDtypeStruct((rows_each, cols_each), F32),
+        scratch_shapes=[
+            pltpu.VMEM((groups, rows_each, feat), F32),
+            pltpu.VMEM((regions, rows_each, feat), F32),
+            pltpu.SemaphoreType.DMA((groups,)),
+            pltpu.SemaphoreType.DMA((groups,)),
+            pltpu.SemaphoreType.DMA((regions,)),
+            pltpu.SemaphoreType.DMA((regions,)),
+        ],
+        compiler_params=pltpu.CompilerParams(collective_id=0, has_side_effects=True),
+        cost_estimate=pl.CostEstimate(
+            flops=6 * rows_each * cols_each * feat, bytes_accessed=1 << 20, transcendentals=0
+        ),
+        name="reduce_gradient",
+    )(sym, model_coefficients)
     return (link.reshape(count), grad)
 
 

time: 232 us -> 104 us (0.45)
  waiting for transfers between devices: 142 us -> 0 us
  Pallas kernels: 60.9 us -> 95.5 us
  between operations: 14.1 us -> 0.67 us
  local copies, waits for them, and re-layouts: 9.13 us -> 5.44 us
    psum x1 -> x0, waiting for transfers between devices: 124 us -> none  [body(): sym = lax.psum(sym, ('block', 'geo'))]
    all_gather x1 -> x0, waiting for transfers between devices: 18.8 us -> none  [body(): lax.all_gather(jnp.concatenate([population_vectors, census_code], axis=0)...]
    pallas_call x1, Pallas kernels: 30.1 us -> 47.7 us  [body(): pl.pallas_call(functools.partial(order_kernel, groups, cap), grid=(groups...]
    pallas_call x0 -> x1, Pallas kernels: none -> 17.1 us  [body(): pl.pallas_call(functools.partial(reduce_kernel, groups, regions), in_spec...]
    unnamed x16 -> x11, local copies, waits for them, and re-layouts: 9.12 us -> 5.42 us
  transfers between devices with their start and end apart: 2 -> 0, of which waited for: 2 -> 0; matrix products, arithmetic and copies ran while one was open for 0% -> 0% of each run, Pallas kernels for 13% -> 0%
where the time goes in v2:
time: 104 us
  Pallas kernels  95.5 us (92%)
  local copies, waits for them, and re-layouts  5.44 us (5%)
  other arithmetic  2.41 us (2%)
    pallas_call x1, Pallas kernels, body(): pl.pallas_call(functools.partial(order_kernel, groups, cap), grid=(groups...  47.7 us
    pallas_call x1, Pallas kernels, body(): pl.pallas_call(functools.partial(score_kernel, groups, cap, grad_scale),...  30.7 us
    pallas_call x1, Pallas kernels, body(): pl.pallas_call(functools.partial(reduce_kernel, groups, regions), in_spec...  17.1 us
    unnamed x11, local copies, waits for them, and re-layouts  5.42 us

profile of v2, /device:TPU:0, one launch (start us, length us, event | category | flops | bytes accessed | tf_op | source)
XLA Modules:
  0.0 104.0 jit_solution(331600074819557320)
XLA Ops:
  0.6 0.7 add_convert_fusion.1
  1.4 0.7 add_convert_fusion
  2.1 1.0 fusion.1.own_ref
  3.1 0.0 copy-start
  3.1 1.0 copy-done
  4.1 0.0 copy-start.3
  4.1 1.6 %copy-done.3 = bf16[4096,256]{1,0:T(8,128)(2,1)S(1)} copy-done((bf16[4096,256]{1,0:T(8,128)(2,1)S(1)}, bf16[4096,256]{1,0:T(8,128)(2,1)}, u32[]{:S(2)}) %copy-start.3) | copy-done | bytes 2097176
  5.7 0.0 copy-start.4
  5.7 0.7 copy-done.4
  6.4 0.0 copy-start.1
  6.4 47.7 %order_records.1 = (bf16[16,384,1024]{2,1,0:T(8,128)(2,1)}, bf16[16,384,256]{2,1,0:T(8,128)(2,1)S(1)}, f32[16,384]{1,0:T(8,128)S(1)}, s32[1,4096]{1,0:T(1,128)S(1)}, bf16[16,528,256]{2,1,0:T(8,128)(2,1)S(1)}) custom-call(s32[1,4096]{1,0:T(1,128)S(1)} %bitcast.4, f32[1,4096]{1,0:T(1,128)S(1)} %bitcast.3, bf16[4096,256]{1,0:T(8,128)(2,1)S(1)} %copy-done.3, ...), custom_call_target="tpu_custom_call" | custom-call | flops 16106127360 | bytes 20971520 | tf_op jit(solution)/shard_map/order_records/pallas_call | solution.py:305
  54.2 0.0 copy-done.1
  54.2 30.7 %score_pairs.1 = (f32[1,4096]{1,0:T(1,128)}, f32[256,256]{1,0:T(8,128)S(1)}) custom-call(s32[1,4096]{1,0:T(1,128)S(1)} %bitcast.5, s32[1,4096]{1,0:T(1,128)S(1)} %get-tuple-element.9.rank_ref, f32[16,384]{1,0:T(8,128)S(1)} %get-tuple-element.10.slots_ref, bf16[256,1024]{1,0:T(8,128)(2,1)S(1)} %copy-done.1, ...), custom_call_target="tpu_custom_call" | custom-call | flops 14495514624 | bytes 20971520 | tf_op jit(solution)/shard_map/score_pairs/pallas_call | solution.py:332
  84.9 0.0 copy-start.2
  84.9 0.7 copy-done.2
  85.6 17.1 %reduce_gradient.1 = f32[16,512]{1,0:T(8,128)} custom-call(f32[256,256]{1,0:T(8,128)} %copy-done.2, bf16[256,1024]{1,0:T(8,128)(2,1)} %m_ref.5), custom_call_target="tpu_custom_call" | custom-call | flops 12582912 | bytes 1048576 | tf_op jit(solution)/shard_map/reduce_gradient/pallas_call | solution.py:358
  102.6 1.4 %copy.11 = f32[16,512]{1,0:T(8,128)} copy(f32[16,512]{1,0:T(8,128)} %reduce_gradient.1) | data formatting | bytes 65536
  (1 shorter events, 0.0 us)
Async XLA Ops:
  3.1 1.0 %copy-start = (bf16[256,1024]{1,0:T(8,128)(2,1)S(1)}, bf16[256,1024]{1,0:T(8,128)(2,1)}, u32[]{:S(2)}) copy-start(bf16[256,1024]{1,0:T(8,128)(2,1)} %m_ref.5) | copy-start | bytes 1572868
  4.1 1.6 %copy-start.3 = (bf16[4096,256]{1,0:T(8,128)(2,1)S(1)}, bf16[4096,256]{1,0:T(8,128)(2,1)}, u32[]{:S(2)}) copy-start(bf16[4096,256]{1,0:T(8,128)(2,1)} %x_ref.1) | copy-start | bytes 6291460
  5.7 0.7 copy-start.4
  6.4 47.7 %copy-start.1 = (bf16[256,1024]{1,0:T(8,128)(2,1)S(1)}, bf16[256,1024]{1,0:T(8,128)(2,1)}, u32[]{:S(2)}) copy-start(bf16[256,1024]{1,0:T(8,128)(2,1)} %m_ref.5) | copy-start | bytes 1572868
  84.9 0.7 copy-start.2

commit v3 on v2

--- a/solution.py
+++ b/solution.py
@@ -87,7 +87,7 @@
 
     for k in range(1, outer):
 
-        @pl.when(step == (2, 6, 8, 10)[k])
+        @pl.when(step == (0, 10, 11, 12)[k])
         def _(k=k):
             along_outer(k).wait_recv()
             for j in range(1, inner):
@@ -96,31 +96,42 @@
 
     for k in range(outer):
 
-        @pl.when(step == (7, 10, 12, 14)[k])
+        @pl.when(step == (5, groups + 2, groups + 4, groups + 6)[k])
         def _(k=k):
             for j in range(1, inner):
                 along_inner(k, j).wait_recv()
                 to_core(k, j).start()
 
-    @pl.when(step == groups - 1)
+    @pl.when(step == groups)
     def _():
         pltpu.make_async_copy(own_ref, all_ref.at[block], local).wait()
+
+    for k in range(outer):
+        for j in range(inner):
+
+            @pl.when(step == groups + j * 2 * outer + 2 * k + 1)
+            def _(k=k, j=j):
+                to_core(k, j).wait_recv()
+
+    @pl.when(step == 2 * groups - 1)
+    def _():
         for k in range(1, outer):
             along_outer(k).wait_send()
         for k in range(outer):
             for j in range(1, inner):
                 along_inner(k, j).wait_send()
             for j in range(inner):
-                to_core(k, j).wait()
-
-
-def order_kernel(
-    groups, cap, dest_ref, code_ref, x_ref, m_ref, own_ref, proj_ref, rows_ref, slots_ref, rank_ref, all_ref,
-    local, *sems,
-):
-    owner = pl.program_id(0)
+                to_core(k, j).wait_send()
+
+    turn = jnp.maximum(step - groups, 0)
+    z = lax.rem(block // (2 * inner) + outer - lax.rem(turn // 2, outer), outer)
+    x = lax.rem(lax.rem(block // 2, inner) + inner - turn // (2 * outer), inner)
+    core = lax.rem(lax.rem(block, 2) + turn, 2)
+    return (z * inner + x) * 2 + core
+
+
+def order_rows(groups, cap, owner, dest_ref, code_ref, x_ref, m_ref, proj_ref, rows_ref, slots_ref, rank_ref):
     count = dest_ref.shape[1]
-    gather_step(groups, owner, own_ref, all_ref, local, *sems)
 
     @pl.when(owner == 0)
     def _():
@@ -151,23 +162,22 @@
         placed = jnp.where(places == mine, 1.0, 0.0).astype(BF16)
         rows = rows + plain(placed, x_ref[span, :])
     rows = rows.astype(BF16)
-    rows_ref[0] = rows
-    proj_ref[0] = plain(rows, m_ref[...]).astype(BF16)
-
-
-def score_kernel(
-    groups, cap, grad_scale,
+    rows_ref[owner] = rows
+    proj_ref[owner] = plain(rows, m_ref[...]).astype(BF16)
+
+
+def score_block(
+    groups, cap, grad_scale, turn, owner,
     dest_ref, rank_ref, slots_ref, m_ref, proj_ref, rows_ref, census_ref,
     link_ref, sym_ref, total_ref, sums_ref,
 ):
-    owner = pl.program_id(0)
     count = dest_ref.shape[1]
     feat = rows_ref.shape[2]
     hidden = m_ref.shape[1]
-    people = census_ref.shape[1] // 16 * 16 - 16
-
-    census = census_ref[0, :people, :]
-    labels = census_ref[0, people:, :].astype(F32)
+    people = census_ref.shape[1] - 16
+
+    census = census_ref[owner, :people, :]
+    labels = census_ref[owner, people:, :].astype(F32)
     columns = []
     for part in range(people // feat):
         row = jnp.broadcast_to(labels[part : part + 1, :], (128, feat))
@@ -178,25 +188,25 @@
     slot_key = jnp.floor((slot_label - 1.0) * 0.25)
 
     mapped = plain(census, m_ref[...]).astype(BF16)
-    raw = over_columns(mapped, proj_ref[0])
+    raw = over_columns(mapped, proj_ref[owner])
     prob = 0.5 * jnp.tanh(raw * (0.5 / hidden**0.5)) + 0.5
     prob = jnp.where(key == slot_key, prob, 0.0)
     sums_ref[pl.ds(owner, 1), :] = jnp.sum(prob, axis=0, keepdims=True)
     resid = (prob - jnp.where(label == slot_label, 1.0, 0.0)).astype(BF16)
-    pulled = plain(resid, rows_ref[0])
+    pulled = plain(resid, rows_ref[owner])
     high = pulled.astype(BF16)
     low = (pulled - high.astype(F32)).astype(BF16)
     step = over_rows(census, high) + over_rows(census, low)
 
-    @pl.when(owner == 0)
+    @pl.when(turn == 0)
     def _():
         total_ref[...] = step
 
-    @pl.when(owner > 0)
+    @pl.when(turn > 0)
     def _():
         total_ref[...] += step
 
-    @pl.when(owner == groups - 1)
+    @pl.when(turn == groups - 1)
     def _():
         total = total_ref[...]
         sym_ref[...] = (total + jnp.transpose(total)) * grad_scale
@@ -211,6 +221,28 @@
             spread = over_rows(top, onehot) + over_rows(rest, onehot)
             spread = jnp.where(places == rank_ref[:, span], spread, 0.0)
             link_ref[:, span] = jnp.sum(spread, axis=0, keepdims=True)
+
+
+def link_kernel(
+    groups, cap, grad_scale, dest_ref, code_ref, x_ref, m_ref, own_ref, link_ref, sym_ref,
+    proj_ref, rows_ref, slots_ref, rank_ref, all_ref, total_ref, sums_ref, local, *sems,
+):
+    step = pl.program_id(0)
+    owner = gather_step(groups, step, own_ref, all_ref, local, *sems)
+
+    @pl.when(step < groups)
+    def _():
+        order_rows(
+            groups, cap, step, dest_ref, code_ref, x_ref, m_ref, proj_ref, rows_ref, slots_ref, rank_ref
+        )
+
+    @pl.when(step >= groups)
+    def _():
+        score_block(
+            groups, cap, grad_scale, step - groups, owner,
+            dest_ref, rank_ref, slots_ref, m_ref, proj_ref, rows_ref, all_ref,
+            link_ref, sym_ref, total_ref, sums_ref,
+        )
 
 
 def reduce_kernel(groups, regions, sym_ref, m_ref, grad_ref, got, mid, send1, recv1, send2, recv2):
@@ -299,59 +331,37 @@
     def whole(shape):
         return pl.BlockSpec(shape, lambda o: (0,) * len(shape))
 
-    def each(shape):
-        return pl.BlockSpec((1,) + shape, lambda o: (o, 0, 0))
-
-    proj, rows, slots, rank, census = pl.pallas_call(
-        functools.partial(order_kernel, groups, cap),
-        grid=(groups,),
+    grad_scale = 1.0 / hidden**0.5 / (count * groups * regions) ** 0.5
+    link, sym = pl.pallas_call(
+        functools.partial(link_kernel, groups, cap, grad_scale),
+        grid=(2 * groups,),
         in_specs=[whole((1, count)), whole((1, count)), whole((count, feat)), whole((feat, hidden))]
         + [pl.BlockSpec(memory_space=pl.ANY)],
-        out_specs=[each((cap, hidden)), each((cap, feat)), whole((groups, cap)), whole((1, count))]
-        + [pl.BlockSpec(memory_space=pl.ANY)],
-        out_shape=[
-            jax.ShapeDtypeStruct((groups, cap, hidden), BF16),
-            jax.ShapeDtypeStruct((groups, cap, feat), BF16),
-            jax.ShapeDtypeStruct((groups, cap), F32),
-            jax.ShapeDtypeStruct((1, count), jnp.int32),
-            jax.ShapeDtypeStruct((groups, tall, feat), BF16),
-        ],
-        scratch_shapes=[pltpu.SemaphoreType.DMA]
+        out_specs=[whole((1, count)), whole((feat, feat))],
+        out_shape=[jax.ShapeDtypeStruct((1, count), F32), jax.ShapeDtypeStruct((feat, feat), F32)],
+        scratch_shapes=[
+            pltpu.VMEM((groups, cap, hidden), BF16),
+            pltpu.VMEM((groups, cap, feat), BF16),
+            pltpu.VMEM((groups, cap), F32),
+            pltpu.VMEM((1, count), jnp.int32),
+            pltpu.VMEM((groups, tall, feat), BF16),
+            pltpu.VMEM((feat, feat), F32),
+            pltpu.VMEM((groups, cap), F32),
+            pltpu.SemaphoreType.DMA,
+        ]
         + [pltpu.SemaphoreType.DMA((4,))] * 2
         + [pltpu.SemaphoreType.DMA((groups // 2,))] * 4,
         compiler_params=pltpu.CompilerParams(
-            vmem_limit_bytes=40 << 20, collective_id=1, has_side_effects=True
+            vmem_limit_bytes=48 << 20, collective_id=1, has_side_effects=True
         ),
         cost_estimate=pl.CostEstimate(
-            flops=2 * groups * cap * feat * (count + hidden), bytes_accessed=20 << 20, transcendentals=0
-        ),
-        name="order_records",
-    )(dest, code, admin_vectors, model_coefficients, census)
-
-    grad_scale = 1.0 / hidden**0.5 / (count * groups * regions) ** 0.5
-    link, sym = pl.pallas_call(
-        functools.partial(score_kernel, groups, cap, grad_scale),
-        grid=(groups,),
-        in_specs=[
-            whole((1, count)),
-            whole((1, count)),
-            whole((groups, cap)),
-            whole((feat, hidden)),
-            each((cap, hidden)),
-            each((cap, feat)),
-            each((tall, feat)),
-        ],
-        out_specs=[whole((1, count)), whole((feat, feat))],
-        out_shape=[jax.ShapeDtypeStruct((1, count), F32), jax.ShapeDtypeStruct((feat, feat), F32)],
-        scratch_shapes=[pltpu.VMEM((feat, feat), F32), pltpu.VMEM((groups, cap), F32)],
-        compiler_params=pltpu.CompilerParams(vmem_limit_bytes=40 << 20),
-        cost_estimate=pl.CostEstimate(
-            flops=2 * groups * people * (feat * hidden + cap * hidden + cap * feat + 2 * feat * feat),
-            bytes_accessed=20 << 20,
+            flops=2 * groups * cap * feat * (count + hidden)
+            + 2 * groups * people * (feat * hidden + cap * hidden + cap * feat + 2 * feat * feat),
+            bytes_accessed=10 << 20,
             transcendentals=groups * people * cap,
         ),
-        name="score_pairs",
-    )(dest, rank, slots, model_coefficients, proj, rows, census)
+        name="link_records",
+    )(dest, code, admin_vectors, model_coefficients, census)
 
     rows_each = feat // groups
     cols_each = hidden // regions

time: 104 us -> 93.8 us (0.902)
  Pallas kernels: 95.5 us -> 83.9 us
    pallas_call x2 -> x1, Pallas kernels: 78.4 us -> 68.8 us  [body(): pl.pallas_call(functools.partial(link_kernel, groups, cap, grad_scale), g...]
    pallas_call x1, Pallas kernels: 17.1 us -> 15 us  [body(): pl.pallas_call(functools.partial(reduce_kernel, groups, regions), in_spec...]
    unnamed x11 -> x10, local copies, waits for them, and re-layouts: 5.42 us -> 6.01 us
where the time goes in v3:
time: 93.8 us; the launch traced here: 93 us
  Pallas kernels  83.9 us (89%)
  local copies, waits for them, and re-layouts  6.03 us (6%)
  other arithmetic  2.41 us (3%)
    pallas_call x1, Pallas kernels, body(): pl.pallas_call(functools.partial(link_kernel, groups, cap, grad_scale), g...  68.8 us
    pallas_call x1, Pallas kernels, body(): pl.pallas_call(functools.partial(reduce_kernel, groups, regions), in_spec...  15 us
    unnamed x10, local copies, waits for them, and re-layouts  6.01 us

profile of v3, /device:TPU:0, one launch (start us, length us, event | category | flops | bytes accessed | tf_op | source)
XLA Modules:
  0.0 93.0 jit_solution(1994483778190422001)
XLA Ops:
  0.6 0.7 add_convert_fusion.1
  1.4 0.7 add_convert_fusion
  2.1 1.0 %fusion.1.own_ref = bf16[528,256]{1,0:T(8,128)(2,1)S(1)} fusion(bf16[2,256]{1,0:T(2,128)(2,1)S(1)} %reshape.18, bf16[512,256]{1,0:T(8,128)(2,1)} %param.12), kind=kLoop, calls=%fused_computation.2 | loop fusion | flops 811008 | bytes 533504 | tf_op jit(solution)/shard_map/concatenate | solution.py:328
  3.1 0.0 copy-start
  3.1 1.0 %copy-done = bf16[256,1024]{1,0:T(8,128)(2,1)S(1)} copy-done((bf16[256,1024]{1,0:T(8,128)(2,1)S(1)}, bf16[256,1024]{1,0:T(8,128)(2,1)}, u32[]{:S(2)}) %copy-start) | copy-done | bytes 524312
  4.1 0.0 copy-start.2
  4.1 1.6 %copy-done.2 = bf16[4096,256]{1,0:T(8,128)(2,1)S(1)} copy-done((bf16[4096,256]{1,0:T(8,128)(2,1)S(1)}, bf16[4096,256]{1,0:T(8,128)(2,1)}, u32[]{:S(2)}) %copy-start.2) | copy-done | bytes 2097176
  5.7 0.0 copy-start.3
  5.7 0.7 copy-done.3
  6.4 68.8 %link_records.1 = (f32[1,4096]{1,0:T(1,128)S(1)}, f32[256,256]{1,0:T(8,128)S(1)}) custom-call(s32[1,4096]{1,0:T(1,128)S(1)} %bitcast.5, f32[1,4096]{1,0:T(1,128)S(1)} %bitcast.3, bf16[4096,256]{1,0:T(8,128)(2,1)S(1)} %copy-done.2, bf16[256,1024]{1,0:T(8,128)(2,1)S(1)} %copy-done, bf16[528,256]{1,0:T(8,128)(2,1)S(1)} %fusion.1.own_ref), custom_call_target="tpu_custom_call" | custom-call | flops 30601641984 | bytes 10485760 | tf_op jit(solution)/shard_map/link_records/pallas_call | solution.py:335
  75.3 0.0 copy-start.1
  75.3 0.7 copy-done.1
  76.0 15.0 %reduce_gradient.1 = f32[16,512]{1,0:T(8,128)} custom-call(f32[256,256]{1,0:T(8,128)} %copy-done.1, bf16[256,1024]{1,0:T(8,128)(2,1)} %m_ref.3), custom_call_target="tpu_custom_call" | custom-call | flops 12582912 | bytes 1048576 | tf_op jit(solution)/shard_map/reduce_gradient/pallas_call | solution.py:368
  91.0 0.6 copy.12
  91.6 1.4 %copy.13 = f32[16,512]{1,0:T(8,128)} copy(f32[16,512]{1,0:T(8,128)} %reduce_gradient.1) | data formatting | bytes 65536
  (1 shorter events, 0.0 us)
Async XLA Ops:
  3.1 1.0 %copy-start = (bf16[256,1024]{1,0:T(8,128)(2,1)S(1)}, bf16[256,1024]{1,0:T(8,128)(2,1)}, u32[]{:S(2)}) copy-start(bf16[256,1024]{1,0:T(8,128)(2,1)} %m_ref.3) | copy-start | bytes 1572868
  4.1 1.6 %copy-start.2 = (bf16[4096,256]{1,0:T(8,128)(2,1)S(1)}, bf16[4096,256]{1,0:T(8,128)(2,1)}, u32[]{:S(2)}) copy-start(bf16[4096,256]{1,0:T(8,128)(2,1)} %x_ref.1) | copy-start | bytes 6291460
  5.7 0.7 copy-start.3
  75.3 0.7 copy-start.1
